TPU v7x, 128 devices: a whole 4x4x4 slice. The times are simulated.
128 devices in a mesh: row: 8 (over z_lo, x), col: 16 (over y, z_hi, core).
Axes of the slice: x: 4, y: 4, z: 4 (z_hi: 2, z_lo: 2; z = z_hi * 2 + z_lo), core: 2. Of those that a mesh axis runs over, the one named last changes fastest.
Arguments:
- anchor_features: float32 [16384, 1024], P(('row', 'col')), may hold values from -6 to 6
- candidate_features: float32 [16384, 1024], P(('row', 'col')), may hold values from -6 to 6
- anchor_sample_ids: int32 [16384], replicated, may hold values from 0 to 4095
- candidate_sample_ids: int32 [16384], replicated, may hold values from 0 to 4095
- opponent_tile: int32 [3, 128], replicated, may hold values from 0 to 127, as said below
- sharpness_array: float32 [1], replicated, may hold values from 8 to 16
- score_offset: float32 [1], replicated, may hold values from -3 to 0
Outputs:
- grad_a: float32 [16384, 1024], P(('row', 'col'))
- grad_b: float32 [16384, 1024], P(('row', 'col'))
Inputs may be any that keep to these rules, and one draw needn't show every extreme that they name: Each row opponent_tile[k] is a perfect pairing of the blocks: opponent_tile[k, opponent_tile[k, q]] = q and opponent_tile[k, q] != q. The 3 rows are consecutive rounds of one round-robin tournament over relabelled blocks, so no two rounds pair the same blocks.
All inputs are finite; a program needn't handle non-finite values.
Results may differ from a plain program's by a relative error of at most 0.0042.
Values may be sent and summed in bfloat16 or wider, within the bound.
A program may use at most 64 MiB of HBM per device.

v0:
```python
import jax
import jax.numpy as jnp
from jax import lax
from jax.sharding import PartitionSpec as P


def normalize(embed):
    sharpness_factor = lax.rsqrt(jnp.sum(embed * embed, axis=-1, keepdims=True) + 1e-06)
    return (embed * sharpness_factor).astype(jnp.bfloat16)


def tile_derivative_fn(
    anchor_tile_vectors,
    candidate_tile_vectors,
    anchor_tile_ids,
    candidate_tile_ids,
    sharpness_array,
    score_offset,
):
    positive_target = jnp.where(
        anchor_tile_ids[:, None] == candidate_tile_ids[None, :], 1.0, -1.0
    ).astype(jnp.float32)
    similarity_score = lax.dot_general(
        anchor_tile_vectors,
        candidate_tile_vectors,
        (((1,), (1,)), ((), ())),
        preferred_element_type=jnp.float32,
    )
    similarity_table = sharpness_array * similarity_score + score_offset
    return (
        -sharpness_array * positive_target * jax.nn.sigmoid(-positive_target * similarity_table)
    ).astype(jnp.bfloat16)


def left_product(slope, operand):
    return lax.dot_general(
        slope, operand, (((0,), (0,)), ((), ())), preferred_element_type=jnp.float32
    )


def route_blocks(block, links):
    count = lax.axis_size(("row", "col"))
    pieces = block.reshape((count, block.shape[0] // count) + block.shape[1:])
    spread = lax.all_to_all(pieces, ("row", "col"), split_axis=0, concat_axis=0, tiled=True)
    spread = jnp.take(spread, links, axis=0)
    landed = lax.all_to_all(spread, ("row", "col"), split_axis=0, concat_axis=0, tiled=True)
    return landed.reshape(block.shape)


def route_grads(block, links):
    count = lax.axis_size(("row", "col"))
    pieces = block.reshape((count, block.shape[0] // count) + block.shape[1:])
    spread = lax.all_to_all(pieces, ("row", "col"), split_axis=0, concat_axis=0, tiled=True)
    spread = jnp.take(spread, links, axis=0)
    landed = lax.all_to_all(spread, ("row", "col"), split_axis=0, concat_axis=0, tiled=True)
    return landed.reshape(block.shape)


def shards(
    anchor_features,
    candidate_features,
    anchor_sample_ids,
    candidate_sample_ids,
    opponent_tile,
    sharpness_array,
    score_offset,
):
    rows = anchor_features.shape[0]
    rounds = opponent_tile.shape[0]
    own_index = lax.axis_index("row") * lax.axis_size("col") + lax.axis_index("col")
    a_hat = normalize(anchor_features)
    b_hat = normalize(candidate_features)
    own_ida = lax.dynamic_slice_in_dim(anchor_sample_ids, own_index * rows, rows)
    own_idb = lax.dynamic_slice_in_dim(candidate_sample_ids, own_index * rows, rows)
    sharpness_factor = sharpness_array[0]
    shift = score_offset[0]
    slope = tile_derivative_fn(a_hat, b_hat, own_ida, own_idb, sharpness_factor, shift)
    total_a = jnp.dot(slope, b_hat, preferred_element_type=jnp.float32)
    total_b = left_product(slope, a_hat)
    for step in range(rounds):
        links = opponent_tile[step]
        other = links[own_index]
        far_idb = lax.dynamic_slice_in_dim(candidate_sample_ids, other * rows, rows)
        far_b = route_blocks(b_hat, links)
        slope = tile_derivative_fn(a_hat, far_b, own_ida, far_idb, sharpness_factor, shift)
        total_a = total_a + jnp.dot(slope, far_b, preferred_element_type=jnp.float32)
        outgoing = left_product(slope, a_hat)
        total_b = total_b + route_grads(outgoing, links)
    return (total_a, total_b)


def solution(mesh):
    placed = (P(("row", "col"), None), P(("row", "col"), None), P(), P(), P(), P(), P())
    return jax.shard_map(
        shards,
        mesh=mesh,
        in_specs=placed,
        out_specs=(P(("row", "col"), None), P(("row", "col"), None)),
        check_vma=False,
    )
```

profile of v0, /device:TPU:0, one launch (start us, length us, event | category | flops | bytes accessed | tf_op | source)
XLA Modules:
  0.0 189.8 jit_solution(2273961248703065294)
XLA Ops:
  0.6 1.2 multiply_reduce_fusion
  3.2 0.9 reshape.225
  4.0 11.1 %all-to-all-start = ((bf16[128,2,512]{2,1,0:T(2,128)(2,1)}), bf16[128,2,512]{2,1,0:T(2,128)(2,1)S(1)}, u32[]{:S(2)}, u32[]{:S(2)}) async-start(bf16[128,2,512]{2,1,0:T(2,128)(2,1)} %reshape.225), calls=%async_computation | async-start | bytes 524288 | tf_op jit(solution)/shard_map/all_to_all | solution.py:44
  15.5 9.9 %all-to-all-done = bf16[128,2,512]{2,1,0:T(2,128)(2,1)S(1)} async-done(((bf16[128,2,512]{2,1,0:T(2,128)(2,1)}), bf16[128,2,512]{2,1,0:T(2,128)(2,1)S(1)}, u32[]{:S(2)}, u32[]{:S(2)}) %all-to-all-start) | async-done | bytes 262176 | tf_op jit(solution)/shard_map/all_to_all | solution.py:44
  27.4 0.9 reshape.231
  28.2 5.3 %all-to-all-start.3 = ((bf16[128,2,512]{2,1,0:T(2,128)(2,1)}), bf16[128,2,512]{2,1,0:T(2,128)(2,1)S(1)}, u32[]{:S(2)}, u32[]{:S(2)}) async-start(bf16[128,2,512]{2,1,0:T(2,128)(2,1)} %reshape.231), calls=%async_computation.3 | async-start | bytes 524288 | tf_op jit(solution)/shard_map/all_to_all | solution.py:46
  42.7 0.9 reshape.229
  43.8 9.5 %all-to-all-start.2 = ((bf16[128,2,512]{2,1,0:T(2,128)(2,1)}), bf16[128,2,512]{2,1,0:T(2,128)(2,1)S(1)}, u32[]{:S(2)}, u32[]{:S(2)}) async-start(bf16[128,2,512]{2,1,0:T(2,128)(2,1)} %reshape.229), calls=%async_computation.2 | async-start | bytes 524288 | tf_op jit(solution)/shard_map/all_to_all | solution.py:46
  57.9 0.9 reshape.227
  59.0 4.5 %all-to-all-done.2 = bf16[128,2,512]{2,1,0:T(2,128)(2,1)S(1)} async-done(((bf16[128,2,512]{2,1,0:T(2,128)(2,1)}), bf16[128,2,512]{2,1,0:T(2,128)(2,1)S(1)}, u32[]{:S(2)}, u32[]{:S(2)}) %all-to-all-start.2) | async-done | bytes 262176 | tf_op jit(solution)/shard_map/all_to_all | solution.py:46
  63.5 5.3 %all-to-all-start.1 = ((bf16[128,2,512]{2,1,0:T(2,128)(2,1)}), bf16[128,2,512]{2,1,0:T(2,128)(2,1)S(1)}, u32[]{:S(2)}, u32[]{:S(2)}) async-start(bf16[128,2,512]{2,1,0:T(2,128)(2,1)} %reshape.227), calls=%async_computation.1 | async-start | bytes 524288 | tf_op jit(solution)/shard_map/all_to_all | solution.py:46
  69.4 1.3 copy.26
  70.8 8.3 %all-to-all-done.1 = bf16[128,2,512]{2,1,0:T(2,128)(2,1)S(1)} async-done(((bf16[128,2,512]{2,1,0:T(2,128)(2,1)}), bf16[128,2,512]{2,1,0:T(2,128)(2,1)S(1)}, u32[]{:S(2)}, u32[]{:S(2)}) %all-to-all-start.1) | async-done | bytes 262176 | tf_op jit(solution)/shard_map/all_to_all | solution.py:46
  79.1 5.3 %all-to-all-start.8 = ((f32[128,1,1024]{2,1,0:T(1,128)}), f32[128,1,1024]{2,1,0:T(1,128)S(1)}, u32[]{:S(2)}, u32[]{:S(2)}) async-start(f32[128,1,1024]{2,1,0:T(1,128)} %copy.26), calls=%async_computation.8 | async-start | bytes 1048576 | tf_op jit(solution)/shard_map/all_to_all | solution.py:53
  85.5 1.4 copy.24
  86.8 10.4 %all-to-all-done.8 = f32[128,1,1024]{2,1,0:T(1,128)S(1)} async-done(((f32[128,1,1024]{2,1,0:T(1,128)}), f32[128,1,1024]{2,1,0:T(1,128)S(1)}, u32[]{:S(2)}, u32[]{:S(2)}) %all-to-all-start.8) | async-done | bytes 524320 | tf_op jit(solution)/shard_map/all_to_all | solution.py:53
  97.2 5.5 %all-to-all-start.6 = ((f32[128,1,1024]{2,1,0:T(1,128)}), f32[128,1,1024]{2,1,0:T(1,128)S(1)}, u32[]{:S(2)}, u32[]{:S(2)}) async-start(f32[128,1,1024]{2,1,0:T(1,128)} %copy.24), calls=%async_computation.6 | async-start | bytes 1048576 | tf_op jit(solution)/shard_map/all_to_all | solution.py:53
  103.8 1.3 copy.22
  105.1 10.4 %all-to-all-done.6 = f32[128,1,1024]{2,1,0:T(1,128)S(1)} async-done(((f32[128,1,1024]{2,1,0:T(1,128)}), f32[128,1,1024]{2,1,0:T(1,128)S(1)}, u32[]{:S(2)}, u32[]{:S(2)}) %all-to-all-start.6) | async-done | bytes 524320 | tf_op jit(solution)/shard_map/all_to_all | solution.py:53
  115.5 5.5 %all-to-all-start.4 = ((f32[128,1,1024]{2,1,0:T(1,128)}), f32[128,1,1024]{2,1,0:T(1,128)S(1)}, u32[]{:S(2)}, u32[]{:S(2)}) async-start(f32[128,1,1024]{2,1,0:T(1,128)} %copy.22), calls=%async_computation.4 | async-start | bytes 1048576 | tf_op jit(solution)/shard_map/all_to_all | solution.py:53
  122.0 1.4 copy.27
  123.4 10.4 %all-to-all-done.4 = f32[128,1,1024]{2,1,0:T(1,128)S(1)} async-done(((f32[128,1,1024]{2,1,0:T(1,128)}), f32[128,1,1024]{2,1,0:T(1,128)S(1)}, u32[]{:S(2)}, u32[]{:S(2)}) %all-to-all-start.4) | async-done | bytes 524320 | tf_op jit(solution)/shard_map/all_to_all | solution.py:53
  133.8 5.5 %all-to-all-start.9 = ((f32[128,1,1024]{2,1,0:T(1,128)}), f32[128,1,1024]{2,1,0:T(1,128)S(1)}, u32[]{:S(2)}, u32[]{:S(2)}) async-start(f32[128,1,1024]{2,1,0:T(1,128)} %copy.27), calls=%async_computation.9 | async-start | bytes 1048576 | tf_op jit(solution)/shard_map/all_to_all | solution.py:55
  140.3 1.3 copy.25
  141.7 10.4 %all-to-all-done.9 = f32[128,1,1024]{2,1,0:T(1,128)S(1)} async-done(((f32[128,1,1024]{2,1,0:T(1,128)}), f32[128,1,1024]{2,1,0:T(1,128)S(1)}, u32[]{:S(2)}, u32[]{:S(2)}) %all-to-all-start.9) | async-done | bytes 524320 | tf_op jit(solution)/shard_map/all_to_all | solution.py:55
  152.1 5.5 %all-to-all-start.7 = ((f32[128,1,1024]{2,1,0:T(1,128)}), f32[128,1,1024]{2,1,0:T(1,128)S(1)}, u32[]{:S(2)}, u32[]{:S(2)}) async-start(f32[128,1,1024]{2,1,0:T(1,128)} %copy.25), calls=%async_computation.7 | async-start | bytes 1048576 | tf_op jit(solution)/shard_map/all_to_all | solution.py:55
  159.9 1.4 copy.23
  161.2 9.1 %all-to-all-done.7 = f32[128,1,1024]{2,1,0:T(1,128)S(1)} async-done(((f32[128,1,1024]{2,1,0:T(1,128)}), f32[128,1,1024]{2,1,0:T(1,128)S(1)}, u32[]{:S(2)}, u32[]{:S(2)}) %all-to-all-start.7) | async-done | bytes 524320 | tf_op jit(solution)/shard_map/all_to_all | solution.py:55
  170.4 5.5 %all-to-all-start.5 = ((f32[128,1,1024]{2,1,0:T(1,128)}), f32[128,1,1024]{2,1,0:T(1,128)S(1)}, u32[]{:S(2)}, u32[]{:S(2)}) async-start(f32[128,1,1024]{2,1,0:T(1,128)} %copy.23), calls=%async_computation.5 | async-start | bytes 1048576 | tf_op jit(solution)/shard_map/all_to_all | solution.py:55
  178.0 1.0 convolution_add_fusion.1
  179.0 9.7 %all-to-all-done.5 = f32[128,1,1024]{2,1,0:T(1,128)S(1)} async-done(((f32[128,1,1024]{2,1,0:T(1,128)}), f32[128,1,1024]{2,1,0:T(1,128)S(1)}, u32[]{:S(2)}, u32[]{:S(2)}) %all-to-all-start.5) | async-done | bytes 524320 | tf_op jit(solution)/shard_map/all_to_all | solution.py:55
  188.7 1.2 fusion.1
  (72 shorter events, 19.0 us)
Async XLA Ops:
  0.6 1.2 copy-start
  3.2 12.1 %copy-start.1 = (f32[128,1024]{1,0:T(8,128)S(1)}, f32[128,1024]{1,0:T(8,128)}, u32[]{:S(2)}) copy-start(f32[128,1024]{1,0:T(8,128)} %param.11) | copy-start | bytes 1572868
  4.0 11.2 %copy-start.8 = (s32[3,128]{1,0:T(4,128)S(1)}, s32[3,128]{1,0:T(4,128)}, u32[]{:S(2)}) copy-start(s32[3,128]{1,0:T(4,128)} %param.15) | copy-start | bytes 4612
  4.0 21.3 %all-to-all-start = ((bf16[128,2,512]{2,1,0:T(2,128)(2,1)}), bf16[128,2,512]{2,1,0:T(2,128)(2,1)S(1)}, u32[]{:S(2)}, u32[]{:S(2)}) async-start(bf16[128,2,512]{2,1,0:T(2,128)(2,1)} %reshape.225), calls=%async_computation | async-start | bytes 524288 | tf_op jit(solution)/shard_map/all_to_all | solution.py:44
  28.2 15.5 %all-to-all-start.3 = ((bf16[128,2,512]{2,1,0:T(2,128)(2,1)}), bf16[128,2,512]{2,1,0:T(2,128)(2,1)S(1)}, u32[]{:S(2)}, u32[]{:S(2)}) async-start(bf16[128,2,512]{2,1,0:T(2,128)(2,1)} %reshape.231), calls=%async_computation.3 | async-start | bytes 524288 | tf_op jit(solution)/shard_map/all_to_all | solution.py:46
  43.8 19.7 %all-to-all-start.2 = ((bf16[128,2,512]{2,1,0:T(2,128)(2,1)}), bf16[128,2,512]{2,1,0:T(2,128)(2,1)S(1)}, u32[]{:S(2)}, u32[]{:S(2)}) async-start(bf16[128,2,512]{2,1,0:T(2,128)(2,1)} %reshape.229), calls=%async_computation.2 | async-start | bytes 524288 | tf_op jit(solution)/shard_map/all_to_all | solution.py:46
  56.2 46.7 %copy-start.9 = (s32[128]{0:T(128)}, s32[128]{0:T(128)S(1)}, u32[]{:S(2)}) copy-start(s32[128]{0:T(128)S(1)} %dynamic_slice.24) | copy-start | bytes 1540
  59.0 10.2 %copy-start.2 = (bf16[128,1,1024]{2,1,0:T(2,128)(2,1)}, bf16[128,1,1024]{2,1,0:T(2,128)(2,1)S(1)}, u32[]{:S(2)}) copy-start(bf16[128,1,1024]{2,1,0:T(2,128)(2,1)S(1)} %reshape.232) | copy-start | bytes 786436
  63.5 15.5 %all-to-all-start.1 = ((bf16[128,2,512]{2,1,0:T(2,128)(2,1)}), bf16[128,2,512]{2,1,0:T(2,128)(2,1)S(1)}, u32[]{:S(2)}, u32[]{:S(2)}) async-start(bf16[128,2,512]{2,1,0:T(2,128)(2,1)} %reshape.227), calls=%async_computation.1 | async-start | bytes 524288 | tf_op jit(solution)/shard_map/all_to_all | solution.py:46
  79.1 18.1 %all-to-all-start.8 = ((f32[128,1,1024]{2,1,0:T(1,128)}), f32[128,1,1024]{2,1,0:T(1,128)S(1)}, u32[]{:S(2)}, u32[]{:S(2)}) async-start(f32[128,1,1024]{2,1,0:T(1,128)} %copy.26), calls=%async_computation.8 | async-start | bytes 1048576 | tf_op jit(solution)/shard_map/all_to_all | solution.py:53
  84.7 0.8 copy-start.4
  97.2 18.3 %all-to-all-start.6 = ((f32[128,1,1024]{2,1,0:T(1,128)}), f32[128,1,1024]{2,1,0:T(1,128)S(1)}, u32[]{:S(2)}, u32[]{:S(2)}) async-start(f32[128,1,1024]{2,1,0:T(1,128)} %copy.24), calls=%async_computation.6 | async-start | bytes 1048576 | tf_op jit(solution)/shard_map/all_to_all | solution.py:53
  103.0 0.8 copy-start.6
  115.5 18.3 %all-to-all-start.4 = ((f32[128,1,1024]{2,1,0:T(1,128)}), f32[128,1,1024]{2,1,0:T(1,128)S(1)}, u32[]{:S(2)}, u32[]{:S(2)}) async-start(f32[128,1,1024]{2,1,0:T(1,128)} %copy.22), calls=%async_computation.4 | async-start | bytes 1048576 | tf_op jit(solution)/shard_map/all_to_all | solution.py:53
  133.8 18.3 %all-to-all-start.9 = ((f32[128,1,1024]{2,1,0:T(1,128)}), f32[128,1,1024]{2,1,0:T(1,128)S(1)}, u32[]{:S(2)}, u32[]{:S(2)}) async-start(f32[128,1,1024]{2,1,0:T(1,128)} %copy.27), calls=%async_computation.9 | async-start | bytes 1048576 | tf_op jit(solution)/shard_map/all_to_all | solution.py:55
  152.1 18.3 %all-to-all-start.7 = ((f32[128,1,1024]{2,1,0:T(1,128)}), f32[128,1,1024]{2,1,0:T(1,128)S(1)}, u32[]{:S(2)}, u32[]{:S(2)}) async-start(f32[128,1,1024]{2,1,0:T(1,128)} %copy.25), calls=%async_computation.7 | async-start | bytes 1048576 | tf_op jit(solution)/shard_map/all_to_all | solution.py:55
  157.6 0.7 copy-start.10
  161.2 14.6 %copy-start.7 = (bf16[128,1,1024]{2,1,0:T(2,128)(2,1)S(1)}, bf16[128,1,1024]{2,1,0:T(2,128)(2,1)}, u32[]{:S(2)}) copy-start(bf16[128,1,1024]{2,1,0:T(2,128)(2,1)} %copy-done.6) | copy-start | bytes 786436
  170.4 18.3 %all-to-all-start.5 = ((f32[128,1,1024]{2,1,0:T(1,128)}), f32[128,1,1024]{2,1,0:T(1,128)S(1)}, u32[]{:S(2)}, u32[]{:S(2)}) async-start(f32[128,1,1024]{2,1,0:T(1,128)} %copy.23), calls=%async_computation.5 | async-start | bytes 1048576 | tf_op jit(solution)/shard_map/all_to_all | solution.py:55
  175.9 1.0 copy-start.5
  176.9 1.0 copy-start.3
where the time goes:
time: 192 us; the launch traced here: 190 us
  waiting for transfers between devices  83.4 us (43%)
  starting transfers between devices  64.2 us (33%)
  local copies, waits for them, and re-layouts  22.8 us (12%)
  between operations  8.47 us (4%)
  other arithmetic  6.23 us (3%)
  matrix products  4.85 us (3%)
    all_to_all x3, waiting for transfers between devices, route_grads(): lax.all_to_all(pieces, ('row', 'col'), split_axis=0, concat_axis=0, tiled...  31.2 us
    all_to_all x3, waiting for transfers between devices, route_grads(): lax.all_to_all(spread, ('row', 'col'), split_axis=0, concat_axis=0, tiled...  29.2 us
    all_to_all x3, starting transfers between devices, route_blocks(): lax.all_to_all(spread, ('row', 'col'), split_axis=0, concat_axis=0, tiled...  20.2 us
    all_to_all x3, starting transfers between devices, route_grads(): lax.all_to_all(spread, ('row', 'col'), split_axis=0, concat_axis=0, tiled...  16.5 us
    all_to_all x3, starting transfers between devices, route_grads(): lax.all_to_all(pieces, ('row', 'col'), split_axis=0, concat_axis=0, tiled...  16.3 us
    all_to_all x3, waiting for transfers between devices, route_blocks(): lax.all_to_all(spread, ('row', 'col'), split_axis=0, concat_axis=0, tiled...  13.1 us
    all_to_all x1, starting transfers between devices, route_blocks(): lax.all_to_all(pieces, ('row', 'col'), split_axis=0, concat_axis=0, tiled...  11.1 us
    all_to_all x1, waiting for transfers between devices, route_blocks(): lax.all_to_all(pieces, ('row', 'col'), split_axis=0, concat_axis=0, tiled...  9.89 us
  transfers between devices with their start and end apart: 10, of which 10 were waited for; matrix products, arithmetic and copies ran while one was open for 12% of the time, Pallas kernels for 0%

commit v1 on v0

v1 whole, which is shorter than its diff:
```python
import functools
import random

import jax
import jax.numpy as jnp
from jax import lax
from jax.experimental import pallas as pl
from jax.experimental.pallas import tpu as pltpu
from jax.sharding import PartitionSpec as P

LOGICAL = pl.DeviceIdType.LOGICAL
CHIPS = 4
TILE = (16, 128)


def far_first():
    offsets = [
        (dx, dy, dz, dc)
        for dx in range(CHIPS)
        for dy in range(CHIPS)
        for dz in range(CHIPS)
        for dc in range(2)
    ][1:]
    random.Random(1).shuffle(offsets)
    offsets.sort(key=lambda o: -sum(min(d, CHIPS - d) for d in o[:3]))
    return offsets


def kernel(
    a_ref,
    b_ref,
    ida_ref,
    idb_ref,
    opponent_ref,
    sharpness_ref,
    offset_ref,
    grad_a_ref,
    grad_b_ref,
    raw,
    own,
    mid,
    out,
    far,
    load_sem,
    send_sem,
    recv_sem,
):
    rounds = opponent_ref.shape[0]
    loads = [
        pltpu.make_async_copy(src, raw.at[side], load_sem.at[side])
        for side, src in enumerate((a_ref, b_ref))
    ]
    for load in loads:
        load.start()

    row, col = lax.axis_index("row"), lax.axis_index("col")
    x, z_lo = row % CHIPS, row // CHIPS
    y, z_hi, core = col // CHIPS, (col // 2) % 2, col % 2
    z = z_hi * 2 + z_lo
    me = row * 16 + col

    xs = [(x + d) % CHIPS for d in range(CHIPS)]
    ys = [(y + d) % CHIPS for d in range(CHIPS)]
    zs = [(z + d) % CHIPS for d in range(CHIPS)]
    cs = [core, 1 - core]
    index_x = [v * 16 for v in xs]
    index_y = [v * 4 for v in ys]
    index_z = [(v % 2) * 64 + (v // 2) * 2 for v in zs]
    group_z = [v * 4 for v in zs]
    group_y = [v * 2 for v in ys]

    def device(o):
        return index_x[o[0]] + index_y[o[1]] + index_z[o[2]] + cs[o[3]]

    def tile_of(o):
        return group_z[o[2]] + xs[o[0]], group_y[o[1]] + cs[o[3]]

    others = far_first()
    barrier = pltpu.get_barrier_semaphore()
    for o in others:
        pl.semaphore_signal(barrier, inc=1, device_id=device(o), device_id_type=LOGICAL)

    for side in range(2):
        loads[side].wait()
        for g in range(8):
            value = raw[side, pl.ds(g * 16, 16), :]
            scale = lax.rsqrt(jnp.sum(value * value, axis=-1, keepdims=True) + 1e-06)
            value = (value * scale).astype(jnp.bfloat16)
            for c in range(8):
                own[side * 8 + g, c] = value[:, c * 128 : (c + 1) * 128]

    pl.semaphore_wait(barrier, len(others))

    for o in others:
        g, c = tile_of(o)
        pltpu.make_async_remote_copy(
            src_ref=own.at[g, c],
            dst_ref=mid.at[me],
            send_sem=send_sem.at[0],
            recv_sem=recv_sem.at[0],
            device_id=device(o),
            device_id_type=LOGICAL,
        ).start()
    my_g, my_c = tile_of((0, 0, 0, 0))
    mid[me] = own[my_g, my_c]

    sharpness = sharpness_ref[0]
    shift = offset_ref[0]

    def block(ref, side, k=None):
        def column(c):
            part = ref[side * 8 : side * 8 + 8, c] if k is None else ref[side * 8 : side * 8 + 8, c, k]
            return part.reshape(128, 128)
        return [jnp.concatenate([column(2 * j), column(2 * j + 1)], axis=1) for j in range(4)]

    def slope(mine, theirs, my_ids, their_ids):
        score = jnp.zeros((128, 128), jnp.float32)
        for p, q in zip(mine, theirs):
            score += lax.dot_general(p, q, (((1,), (1,)), ((), ())), preferred_element_type=jnp.float32)
        label = jnp.where(my_ids == their_ids, 1.0, -1.0).astype(jnp.float32)
        logit = sharpness * score + shift
        return (-sharpness * label * jax.nn.sigmoid(-label * logit)).astype(jnp.bfloat16)

    ids = (ida_ref, idb_ref)
    grads = (grad_a_ref, grad_b_ref)
    my_ids = []
    for side in range(2):
        line = ids[side][pl.ds(me, 1), :]
        my_ids.append(jnp.transpose(jnp.broadcast_to(line, (128, 128))))
    for side in range(2):
        theirs = block(own, 1 - side)
        g = slope(block(own, side), theirs, my_ids[side], ids[1 - side][pl.ds(me, 1), :])
        for j in range(4):
            grads[side][:, j * 256 : (j + 1) * 256] = jnp.dot(g, theirs[j], preferred_element_type=jnp.float32)

    landed = mid.at[pl.ds(0, len(others))]
    pltpu.make_async_copy(landed, landed, recv_sem.at[0]).wait()

    for o in others:
        there = device(o)
        for k in range(rounds):
            out[there, k] = mid[opponent_ref[k, there]]
        pltpu.make_async_remote_copy(
            src_ref=out.at[there],
            dst_ref=far.at[my_g, my_c],
            send_sem=send_sem.at[1],
            recv_sem=recv_sem.at[1],
            device_id=there,
            device_id_type=LOGICAL,
        ).start()
    for k in range(rounds):
        far[my_g, my_c, k] = mid[opponent_ref[k, me]]

    sent = out.at[pl.ds(0, len(others))]
    pltpu.make_async_copy(sent, sent, recv_sem.at[1]).wait()

    for side in range(2):
        mine = block(own, side)
        theirs = [block(far, 1 - side, k) for k in range(rounds)]
        g = jnp.concatenate(
            [
                slope(mine, theirs[k], my_ids[side], ids[1 - side][pl.ds(opponent_ref[k, me], 1), :])
                for k in range(rounds)
            ],
            axis=1,
        )
        for j in range(4):
            slab = jnp.concatenate([theirs[k][j] for k in range(rounds)], axis=0)
            grads[side][:, j * 256 : (j + 1) * 256] += jnp.dot(g, slab, preferred_element_type=jnp.float32)

    pltpu.make_async_copy(landed, landed, send_sem.at[0]).wait()
    pltpu.make_async_copy(sent, sent, send_sem.at[1]).wait()


def shards(
    anchor_features,
    candidate_features,
    anchor_sample_ids,
    candidate_sample_ids,
    opponent_tile,
    sharpness_array,
    score_offset,
):
    rows, width = anchor_features.shape
    rounds, blocks = opponent_tile.shape
    anywhere = pl.BlockSpec(memory_space=pl.ANY)
    vmem = pl.BlockSpec(memory_space=pltpu.VMEM)
    smem = pl.BlockSpec(memory_space=pltpu.SMEM)
    grad = jax.ShapeDtypeStruct((rows, width), jnp.float32)
    return pl.pallas_call(
        kernel,
        out_shape=(grad, grad),
        in_specs=[anywhere, anywhere, vmem, vmem, smem, smem, smem],
        out_specs=(vmem, vmem),
        scratch_shapes=[
            pltpu.VMEM((2, rows, width), jnp.float32),
            pltpu.VMEM((16, 8) + TILE, jnp.bfloat16),
            pltpu.VMEM((blocks,) + TILE, jnp.bfloat16),
            pltpu.VMEM((blocks, rounds) + TILE, jnp.bfloat16),
            pltpu.VMEM((16, 8, rounds) + TILE, jnp.bfloat16),
            pltpu.SemaphoreType.DMA((2,)),
            pltpu.SemaphoreType.DMA((2,)),
            pltpu.SemaphoreType.DMA((2,)),
        ],
        compiler_params=pltpu.CompilerParams(
            collective_id=0, has_side_effects=True, vmem_limit_bytes=32 * 1024 * 1024
        ),
        name="spread_deliver",
    )(
        anchor_features,
        candidate_features,
        anchor_sample_ids.reshape(blocks, rows),
        candidate_sample_ids.reshape(blocks, rows),
        opponent_tile,
        sharpness_array,
        score_offset,
    )


def solution(mesh):
    placed = (P(("row", "col"), None), P(("row", "col"), None), P(), P(), P(), P(), P())
    return jax.shard_map(
        shards,
        mesh=mesh,
        in_specs=placed,
        out_specs=(P(("row", "col"), None), P(("row", "col"), None)),
        check_vma=False,
    )
```

time: 192 us -> 49.4 us (0.26)
  the two profiles are of different devices: /device:TPU:0 before, /device:TPU:1 now
where the time goes in v1:
time: 49.4 us; the launch traced here: 49.1 us
  Pallas kernels  41.1 us (83%)
  local copies, waits for them, and re-layouts  6.02 us (12%)
  between operations  1.94 us (4%)
    pallas_call x1, Pallas kernels, shards(): pl.pallas_call(kernel, out_shape=(grad, grad), in_specs=[anywhere, anywhe...  41.1 us
    unnamed x12, local copies, waits for them, and re-layouts  6.02 us

profile of v1, /device:TPU:1, one launch (start us, length us, event | category | flops | bytes accessed | tf_op | source)
XLA Modules:
  0.0 49.1 jit_solution(18338955846195896285)
XLA Ops:
  1.9 0.0 copy-start.4
  1.9 0.7 %copy-done.4 = s32[3,128]{1,0:T(4,128)S(1)} copy-done((s32[3,128]{1,0:T(4,128)S(1)}, s32[3,128]{1,0:T(4,128)}, u32[]{:S(2)}) %copy-start.4) | copy-done | bytes 1560
  2.6 0.0 copy-start
  2.6 1.0 %copy-done = f32[128,1024]{1,0:T(8,128)S(1)} copy-done((f32[128,1024]{1,0:T(8,128)S(1)}, f32[128,1024]{1,0:T(8,128)}, u32[]{:S(2)}) %copy-start) | copy-done | bytes 524312
  3.6 0.0 copy-start.1
  3.6 1.0 %copy-done.1 = f32[128,1024]{1,0:T(8,128)S(1)} copy-done((f32[128,1024]{1,0:T(8,128)S(1)}, f32[128,1024]{1,0:T(8,128)}, u32[]{:S(2)}) %copy-start.1) | copy-done | bytes 524312
  4.7 0.0 copy-start.2
  4.7 0.8 %copy-done.2 = s32[16384]{0:T(1024)S(1)} copy-done((s32[16384]{0:T(1024)S(1)}, s32[16384]{0:T(1024)}, u32[]{:S(2)}) %copy-start.2) | copy-done | bytes 65560
  5.5 0.0 copy-start.3
  5.5 0.8 %copy-done.3 = s32[16384]{0:T(1024)S(1)} copy-done((s32[16384]{0:T(1024)S(1)}, s32[16384]{0:T(1024)}, u32[]{:S(2)}) %copy-start.3) | copy-done | bytes 65560
  6.4 41.1 %spread_deliver.1 = (f32[128,1024]{1,0:T(8,128)S(1)}, f32[128,1024]{1,0:T(8,128)S(1)}) custom-call(f32[128,1024]{1,0:T(8,128)S(1)} %copy-done, f32[128,1024]{1,0:T(8,128)S(1)} %copy-done.1, s32[128,128]{1,0:T(8,128)S(1)} %bitcast.2, s32[128,128]{1,0:T(8,128)S(1)} %bitcast.3, s32[3,128]{1,0:T(4,128)S(1)} %copy-done.4, f32[1]{0:T(128)S(6)} %copy.11.sharpness_ref, ...), custom_call_target="tpu_custom_call" | custom-call | tf_op jit(solution)/shard_map/spread_deliver/pallas_call | solution.py:190
  47.5 0.8 %copy.13 = f32[128,1024]{1,0:T(8,128)} copy(f32[128,1024]{1,0:T(8,128)S(1)} %get-tuple-element.4) | data formatting | bytes 1048576
  48.3 0.8 %copy.14 = f32[128,1024]{1,0:T(8,128)} copy(f32[128,1024]{1,0:T(8,128)S(1)} %get-tuple-element.5) | data formatting | bytes 1048576
Async XLA Ops:
  1.9 0.7 %copy-start.4 = (s32[3,128]{1,0:T(4,128)S(1)}, s32[3,128]{1,0:T(4,128)}, u32[]{:S(2)}) copy-start(s32[3,128]{1,0:T(4,128)} %opponent_ref.1) | copy-start | bytes 4612
  2.6 1.0 %copy-start = (f32[128,1024]{1,0:T(8,128)S(1)}, f32[128,1024]{1,0:T(8,128)}, u32[]{:S(2)}) copy-start(f32[128,1024]{1,0:T(8,128)} %a_ref.1) | copy-start | bytes 1572868
  3.6 1.0 %copy-start.1 = (f32[128,1024]{1,0:T(8,128)S(1)}, f32[128,1024]{1,0:T(8,128)}, u32[]{:S(2)}) copy-start(f32[128,1024]{1,0:T(8,128)} %b_ref.1) | copy-start | bytes 1572868
  4.7 0.8 %copy-start.2 = (s32[16384]{0:T(1024)S(1)}, s32[16384]{0:T(1024)}, u32[]{:S(2)}) copy-start(s32[16384]{0:T(1024)} %param.9) | copy-start | bytes 196612
  5.5 0.8 %copy-start.3 = (s32[16384]{0:T(1024)S(1)}, s32[16384]{0:T(1024)}, u32[]{:S(2)}) copy-start(s32[16384]{0:T(1024)} %param.10) | copy-start | bytes 196612

commit v2 on v1

--- a/solution.py
+++ b/solution.py
@@ -11,6 +11,10 @@
 LOGICAL = pl.DeviceIdType.LOGICAL
 CHIPS = 4
 TILE = (16, 128)
+
+
+def in_hbm(array):
+    return pltpu.with_memory_space_constraint(array, pltpu.HBM)
 
 
 def far_first():
@@ -31,12 +35,14 @@
     b_ref,
     ida_ref,
     idb_ref,
-    opponent_ref,
+    opponent_hbm,
     sharpness_ref,
     offset_ref,
     grad_a_ref,
     grad_b_ref,
     raw,
+    ids,
+    opponent_ref,
     own,
     mid,
     out,
@@ -47,8 +53,16 @@
 ):
     rounds = opponent_ref.shape[0]
     loads = [
-        pltpu.make_async_copy(src, raw.at[side], load_sem.at[side])
-        for side, src in enumerate((a_ref, b_ref))
+        pltpu.make_async_copy(src, dst, load_sem.at[i])
+        for i, (src, dst) in enumerate(
+            (
+                (a_ref, raw.at[0]),
+                (b_ref, raw.at[1]),
+                (ida_ref, ids.at[0]),
+                (idb_ref, ids.at[1]),
+                (opponent_hbm, opponent_ref),
+            )
+        )
     ]
     for load in loads:
         load.start()
@@ -121,15 +135,16 @@
         logit = sharpness * score + shift
         return (-sharpness * label * jax.nn.sigmoid(-label * logit)).astype(jnp.bfloat16)
 
-    ids = (ida_ref, idb_ref)
+    for load in loads[2:]:
+        load.wait()
     grads = (grad_a_ref, grad_b_ref)
     my_ids = []
     for side in range(2):
-        line = ids[side][pl.ds(me, 1), :]
+        line = ids[side, pl.ds(me, 1), :]
         my_ids.append(jnp.transpose(jnp.broadcast_to(line, (128, 128))))
     for side in range(2):
         theirs = block(own, 1 - side)
-        g = slope(block(own, side), theirs, my_ids[side], ids[1 - side][pl.ds(me, 1), :])
+        g = slope(block(own, side), theirs, my_ids[side], ids[1 - side, pl.ds(me, 1), :])
         for j in range(4):
             grads[side][:, j * 256 : (j + 1) * 256] = jnp.dot(g, theirs[j], preferred_element_type=jnp.float32)
 
@@ -159,7 +174,7 @@
         theirs = [block(far, 1 - side, k) for k in range(rounds)]
         g = jnp.concatenate(
             [
-                slope(mine, theirs[k], my_ids[side], ids[1 - side][pl.ds(opponent_ref[k, me], 1), :])
+                slope(mine, theirs[k], my_ids[side], ids[1 - side, pl.ds(opponent_ref[k, me], 1), :])
                 for k in range(rounds)
             ],
             axis=1,
@@ -183,22 +198,24 @@
 ):
     rows, width = anchor_features.shape
     rounds, blocks = opponent_tile.shape
-    anywhere = pl.BlockSpec(memory_space=pl.ANY)
+    hbm = pl.BlockSpec(memory_space=pltpu.HBM)
     vmem = pl.BlockSpec(memory_space=pltpu.VMEM)
     smem = pl.BlockSpec(memory_space=pltpu.SMEM)
     grad = jax.ShapeDtypeStruct((rows, width), jnp.float32)
     return pl.pallas_call(
         kernel,
         out_shape=(grad, grad),
-        in_specs=[anywhere, anywhere, vmem, vmem, smem, smem, smem],
+        in_specs=[hbm, hbm, hbm, hbm, hbm, smem, smem],
         out_specs=(vmem, vmem),
         scratch_shapes=[
             pltpu.VMEM((2, rows, width), jnp.float32),
+            pltpu.VMEM((2, blocks, rows), jnp.int32),
+            pltpu.SMEM((rounds, blocks), jnp.int32),
             pltpu.VMEM((16, 8) + TILE, jnp.bfloat16),
             pltpu.VMEM((blocks,) + TILE, jnp.bfloat16),
             pltpu.VMEM((blocks, rounds) + TILE, jnp.bfloat16),
             pltpu.VMEM((16, 8, rounds) + TILE, jnp.bfloat16),
-            pltpu.SemaphoreType.DMA((2,)),
+            pltpu.SemaphoreType.DMA((5,)),
             pltpu.SemaphoreType.DMA((2,)),
             pltpu.SemaphoreType.DMA((2,)),
         ],
@@ -207,11 +224,11 @@
         ),
         name="spread_deliver",
     )(
-        anchor_features,
-        candidate_features,
-        anchor_sample_ids.reshape(blocks, rows),
-        candidate_sample_ids.reshape(blocks, rows),
-        opponent_tile,
+        in_hbm(anchor_features),
+        in_hbm(candidate_features),
+        in_hbm(anchor_sample_ids.reshape(blocks, rows)),
+        in_hbm(candidate_sample_ids.reshape(blocks, rows)),
+        in_hbm(opponent_tile),
         sharpness_array,
         score_offset,
     )

time: 49.4 us -> 44.2 us (0.89)
  local copies, waits for them, and re-layouts: 6.02 us -> 1.59 us
  Pallas kernels: 41.1 us -> 40.6 us
    unnamed x12 -> x2, local copies, waits for them, and re-layouts: 6.02 us -> 1.59 us
    pallas_call x1, Pallas kernels: 41.1 us -> 40.6 us  [shards(): pl.pallas_call(kernel, out_shape=(grad, grad), in_specs=[hbm, hbm, hbm, h...]
where the time goes in v2:
time: 44.2 us; the launch traced here: 44.1 us
  Pallas kernels  40.6 us (92%)
  between operations  1.93 us (4%)
  local copies, waits for them, and re-layouts  1.59 us (4%)
    pallas_call x1, Pallas kernels, shards(): pl.pallas_call(kernel, out_shape=(grad, grad), in_specs=[hbm, hbm, hbm, h...  40.6 us
    unnamed x2, local copies, waits for them, and re-layouts  1.59 us

profile of v2, /device:TPU:1, one launch (start us, length us, event | category | flops | bytes accessed | tf_op | source)
XLA Modules:
  0.0 44.1 jit_solution(2784712847094797640)
XLA Ops:
  1.9 40.6 %spread_deliver.1 = (f32[128,1024]{1,0:T(8,128)S(1)}, f32[128,1024]{1,0:T(8,128)S(1)}) custom-call(f32[128,1024]{1,0:T(8,128)} %a_ref.1, f32[128,1024]{1,0:T(8,128)} %b_ref.1, s32[128,128]{1,0:T(8,128)} %bitcast.2, s32[128,128]{1,0:T(8,128)} %bitcast.3, s32[3,128]{1,0:T(4,128)} %opponent_hbm.1, f32[1]{0:T(128)S(6)} %copy.11.sharpness_ref, f32[1]{0:T(128)S(6)} %copy.12.offset_ref), custom_call_target="tpu_custom_call" | custom-call | tf_op jit(solution)/shard_map/spread_deliver/pallas_call | solution.py:205
  42.5 0.8 %copy.13 = f32[128,1024]{1,0:T(8,128)} copy(f32[128,1024]{1,0:T(8,128)S(1)} %get-tuple-element.4) | data formatting | bytes 1048576
  43.3 0.8 %copy.14 = f32[128,1024]{1,0:T(8,128)} copy(f32[128,1024]{1,0:T(8,128)S(1)} %get-tuple-element.5) | data formatting | bytes 1048576

commit v3 on v2

--- a/solution.py
+++ b/solution.py
@@ -18,15 +18,9 @@
 
 
 def far_first():
-    offsets = [
-        (dx, dy, dz, dc)
-        for dx in range(CHIPS)
-        for dy in range(CHIPS)
-        for dz in range(CHIPS)
-        for dc in range(2)
-    ][1:]
+    offsets = [(dx, dy, dz) for dx in range(CHIPS) for dy in range(CHIPS) for dz in range(CHIPS)][1:]
     random.Random(1).shuffle(offsets)
-    offsets.sort(key=lambda o: -sum(min(d, CHIPS - d) for d in o[:3]))
+    offsets.sort(key=lambda o: -sum(min(d, CHIPS - d) for d in o))
     return offsets
 
 
@@ -76,22 +70,25 @@
     xs = [(x + d) % CHIPS for d in range(CHIPS)]
     ys = [(y + d) % CHIPS for d in range(CHIPS)]
     zs = [(z + d) % CHIPS for d in range(CHIPS)]
-    cs = [core, 1 - core]
     index_x = [v * 16 for v in xs]
     index_y = [v * 4 for v in ys]
     index_z = [(v % 2) * 64 + (v // 2) * 2 for v in zs]
-    group_z = [v * 4 for v in zs]
-    group_y = [v * 2 for v in ys]
+    group_x = [v // 2 for v in xs]
+    group_z = [v * 2 for v in zs]
+    column_x = [(v % 2) * 4 for v in xs]
 
     def device(o):
-        return index_x[o[0]] + index_y[o[1]] + index_z[o[2]] + cs[o[3]]
+        return index_x[o[0]] + index_y[o[1]] + index_z[o[2]] + o[3]
 
     def tile_of(o):
-        return group_z[o[2]] + xs[o[0]], group_y[o[1]] + cs[o[3]]
-
-    others = far_first()
+        return o[3], group_z[o[2]] + group_x[o[0]], column_x[o[0]] + ys[o[1]]
+
+    chips = far_first()
+    here, beside = (0, 0, 0, core), (0, 0, 0, 1 - core)
+    spread = [beside] + [o + (c,) for c in range(2) for o in chips]
+    deliver = [o + (c,) for c in range(2) for o in chips] + [beside]
     barrier = pltpu.get_barrier_semaphore()
-    for o in others:
+    for o in deliver:
         pl.semaphore_signal(barrier, inc=1, device_id=device(o), device_id_type=LOGICAL)
 
     for side in range(2):
@@ -101,29 +98,28 @@
             scale = lax.rsqrt(jnp.sum(value * value, axis=-1, keepdims=True) + 1e-06)
             value = (value * scale).astype(jnp.bfloat16)
             for c in range(8):
-                own[side * 8 + g, c] = value[:, c * 128 : (c + 1) * 128]
-
-    pl.semaphore_wait(barrier, len(others))
-
-    for o in others:
-        g, c = tile_of(o)
+                own[side, g, c] = value[:, c * 128 : (c + 1) * 128]
+
+    pl.semaphore_wait(barrier, len(deliver))
+
+    for o in spread:
         pltpu.make_async_remote_copy(
-            src_ref=own.at[g, c],
+            src_ref=own.at[tile_of(o)],
             dst_ref=mid.at[me],
             send_sem=send_sem.at[0],
             recv_sem=recv_sem.at[0],
             device_id=device(o),
             device_id_type=LOGICAL,
         ).start()
-    my_g, my_c = tile_of((0, 0, 0, 0))
-    mid[me] = own[my_g, my_c]
+    my_tile = tile_of(here)
+    pltpu.make_async_copy(own.at[my_tile], mid.at[me], recv_sem.at[0]).start()
 
     sharpness = sharpness_ref[0]
     shift = offset_ref[0]
 
     def block(ref, side, k=None):
         def column(c):
-            part = ref[side * 8 : side * 8 + 8, c] if k is None else ref[side * 8 : side * 8 + 8, c, k]
+            part = ref[side, :, c] if k is None else ref[side, :, c, k]
             return part.reshape(128, 128)
         return [jnp.concatenate([column(2 * j), column(2 * j + 1)], axis=1) for j in range(4)]
 
@@ -148,28 +144,29 @@
         for j in range(4):
             grads[side][:, j * 256 : (j + 1) * 256] = jnp.dot(g, theirs[j], preferred_element_type=jnp.float32)
 
-    landed = mid.at[pl.ds(0, len(others))]
-    pltpu.make_async_copy(landed, landed, recv_sem.at[0]).wait()
-
-    for o in others:
-        there = device(o)
+    pltpu.make_async_copy(mid, mid, recv_sem.at[0]).wait()
+
+    def fetch(there):
         for k in range(rounds):
             out[there, k] = mid[opponent_ref[k, there]]
+
+    for o in deliver:
+        there = device(o)
+        fetch(there)
         pltpu.make_async_remote_copy(
             src_ref=out.at[there],
-            dst_ref=far.at[my_g, my_c],
+            dst_ref=far.at[my_tile],
             send_sem=send_sem.at[1],
-            recv_sem=recv_sem.at[1],
+            recv_sem=recv_sem.at[1 + core],
             device_id=there,
             device_id_type=LOGICAL,
         ).start()
-    for k in range(rounds):
-        far[my_g, my_c, k] = mid[opponent_ref[k, me]]
-
-    sent = out.at[pl.ds(0, len(others))]
-    pltpu.make_async_copy(sent, sent, recv_sem.at[1]).wait()
-
-    for side in range(2):
+    fetch(me)
+    pltpu.make_async_copy(out.at[me], far.at[my_tile], recv_sem.at[1 + core]).start()
+
+    for side in (1, 0):
+        arrived = far.at[1 - side]
+        pltpu.make_async_copy(arrived, arrived, recv_sem.at[2 - side]).wait()
         mine = block(own, side)
         theirs = [block(far, 1 - side, k) for k in range(rounds)]
         g = jnp.concatenate(
@@ -183,8 +180,21 @@
             slab = jnp.concatenate([theirs[k][j] for k in range(rounds)], axis=0)
             grads[side][:, j * 256 : (j + 1) * 256] += jnp.dot(g, slab, preferred_element_type=jnp.float32)
 
-    pltpu.make_async_copy(landed, landed, send_sem.at[0]).wait()
+    spread_out = mid.at[pl.ds(0, len(spread))]
+    pltpu.make_async_copy(spread_out, spread_out, send_sem.at[0]).wait()
+    sent = out.at[pl.ds(0, len(deliver))]
     pltpu.make_async_copy(sent, sent, send_sem.at[1]).wait()
+
+
+def store(in_a, in_b, out_a, out_b, sem):
+    copies = [
+        pltpu.make_async_copy(src, dst, sem.at[side])
+        for side, (src, dst) in enumerate(((in_a, out_a), (in_b, out_b)))
+    ]
+    for copy in copies:
+        copy.start()
+    for copy in copies:
+        copy.wait()
 
 
 def shards(
@@ -202,7 +212,7 @@
     vmem = pl.BlockSpec(memory_space=pltpu.VMEM)
     smem = pl.BlockSpec(memory_space=pltpu.SMEM)
     grad = jax.ShapeDtypeStruct((rows, width), jnp.float32)
-    return pl.pallas_call(
+    grads = pl.pallas_call(
         kernel,
         out_shape=(grad, grad),
         in_specs=[hbm, hbm, hbm, hbm, hbm, smem, smem],
@@ -211,13 +221,13 @@
             pltpu.VMEM((2, rows, width), jnp.float32),
             pltpu.VMEM((2, blocks, rows), jnp.int32),
             pltpu.SMEM((rounds, blocks), jnp.int32),
-            pltpu.VMEM((16, 8) + TILE, jnp.bfloat16),
+            pltpu.VMEM((2, 8, 8) + TILE, jnp.bfloat16),
             pltpu.VMEM((blocks,) + TILE, jnp.bfloat16),
             pltpu.VMEM((blocks, rounds) + TILE, jnp.bfloat16),
-            pltpu.VMEM((16, 8, rounds) + TILE, jnp.bfloat16),
+            pltpu.VMEM((2, 8, 8, rounds) + TILE, jnp.bfloat16),
             pltpu.SemaphoreType.DMA((5,)),
             pltpu.SemaphoreType.DMA((2,)),
-            pltpu.SemaphoreType.DMA((2,)),
+            pltpu.SemaphoreType.DMA((3,)),
         ],
         compiler_params=pltpu.CompilerParams(
             collective_id=0, has_side_effects=True, vmem_limit_bytes=32 * 1024 * 1024
@@ -232,6 +242,14 @@
         sharpness_array,
         score_offset,
     )
+    return pl.pallas_call(
+        store,
+        out_shape=(grad, grad),
+        in_specs=[vmem, vmem],
+        out_specs=(hbm, hbm),
+        scratch_shapes=[pltpu.SemaphoreType.DMA((2,))],
+        name="store",
+    )(*[pltpu.with_memory_space_constraint(g, pltpu.VMEM) for g in grads])
 
 
 def solution(mesh):

time: 44.2 us -> 41.9 us (0.948)
  local copies, waits for them, and re-layouts: 1.59 us -> 0 us
  Pallas kernels: 40.6 us -> 39.8 us
    pallas_call x1, Pallas kernels: 40.6 us -> 38.8 us  [shards(): pl.pallas_call(kernel, out_shape=(grad, grad), in_specs=[hbm, hbm, hbm, h...]
    unnamed x2 -> x0, local copies, waits for them, and re-layouts: 1.59 us -> none
    pallas_call x0 -> x1, Pallas kernels: none -> 0.99 us  [shards(): pl.pallas_call(store, out_shape=(grad, grad), in_specs=[vmem, vmem], out_...]
where the time goes in v3:
time: 41.9 us; the launch traced here: 41.7 us
  Pallas kernels  39.8 us (95%)
  between operations  1.93 us (5%)
    pallas_call x1, Pallas kernels, shards(): pl.pallas_call(kernel, out_shape=(grad, grad), in_specs=[hbm, hbm, hbm, h...  38.8 us
    pallas_call x1, Pallas kernels, shards(): pl.pallas_call(store, out_shape=(grad, grad), in_specs=[vmem, vmem], out_...  0.99 us

profile of v3, /device:TPU:1, one launch (start us, length us, event | category | flops | bytes accessed | tf_op | source)
XLA Modules:
  0.0 41.7 jit_solution(10700931287189138134)
XLA Ops:
  1.9 38.8 %spread_deliver.1 = (f32[128,1024]{1,0:T(8,128)S(1)}, f32[128,1024]{1,0:T(8,128)S(1)}) custom-call(f32[128,1024]{1,0:T(8,128)} %a_ref.1, f32[128,1024]{1,0:T(8,128)} %b_ref.1, s32[128,128]{1,0:T(8,128)} %bitcast.2, s32[128,128]{1,0:T(8,128)} %bitcast.3, s32[3,128]{1,0:T(4,128)} %opponent_hbm.1, f32[1]{0:T(128)S(6)} %copy.9.sharpness_ref, f32[1]{0:T(128)S(6)} %copy.10.offset_ref), custom_call_target="tpu_custom_call" | custom-call | tf_op jit(solution)/shard_map/spread_deliver/pallas_call | solution.py:215
  40.8 1.0 %store.1 = (f32[128,1024]{1,0:T(8,128)}, f32[128,1024]{1,0:T(8,128)}) custom-call(f32[128,1024]{1,0:T(8,128)S(1)} %get-tuple-element.4.in_a, f32[128,1024]{1,0:T(8,128)S(1)} %get-tuple-element.5.in_b), custom_call_target="tpu_custom_call" | custom-call | tf_op jit(solution)/shard_map/store/pallas_call | solution.py:245

commit v4 on v3

--- a/solution.py
+++ b/solution.py
@@ -86,9 +86,9 @@
     chips = far_first()
     here, beside = (0, 0, 0, core), (0, 0, 0, 1 - core)
     spread = [beside] + [o + (c,) for c in range(2) for o in chips]
-    deliver = [o + (c,) for c in range(2) for o in chips] + [beside]
+    deliver = [o + (c,) for c in (1, 0) for o in chips] + [beside]
     barrier = pltpu.get_barrier_semaphore()
-    for o in deliver:
+    for o in [o + (c,) for o in chips for c in range(2)] + [beside]:
         pl.semaphore_signal(barrier, inc=1, device_id=device(o), device_id_type=LOGICAL)
 
     for side in range(2):

time: 41.9 us -> 41 us (0.979)
  the two profiles are of different devices: /device:TPU:1 before, /device:TPU:0 now
where the time goes in v4:
time: 41 us; the launch traced here: 40.8 us
  Pallas kernels  38.9 us (95%)
  between operations  1.93 us (5%)
    pallas_call x1, Pallas kernels, shards(): pl.pallas_call(kernel, out_shape=(grad, grad), in_specs=[hbm, hbm, hbm, h...  37.9 us
    pallas_call x1, Pallas kernels, shards(): pl.pallas_call(store, out_shape=(grad, grad), in_specs=[vmem, vmem], out_...  0.99 us

profile of v4, /device:TPU:0, one launch (start us, length us, event | category | flops | bytes accessed | tf_op | source)
XLA Modules:
  0.0 40.8 jit_solution(2568449730468510688)
XLA Ops:
  1.9 37.9 %spread_deliver.1 = (f32[128,1024]{1,0:T(8,128)S(1)}, f32[128,1024]{1,0:T(8,128)S(1)}) custom-call(f32[128,1024]{1,0:T(8,128)} %a_ref.1, f32[128,1024]{1,0:T(8,128)} %b_ref.1, s32[128,128]{1,0:T(8,128)} %bitcast.2, s32[128,128]{1,0:T(8,128)} %bitcast.3, s32[3,128]{1,0:T(4,128)} %opponent_hbm.1, f32[1]{0:T(128)S(6)} %copy.9.sharpness_ref, f32[1]{0:T(128)S(6)} %copy.10.offset_ref), custom_call_target="tpu_custom_call" | custom-call | tf_op jit(solution)/shard_map/spread_deliver/pallas_call | solution.py:215
  39.9 1.0 %store.1 = (f32[128,1024]{1,0:T(8,128)}, f32[128,1024]{1,0:T(8,128)}) custom-call(f32[128,1024]{1,0:T(8,128)S(1)} %get-tuple-element.4.in_a, f32[128,1024]{1,0:T(8,128)S(1)} %get-tuple-element.5.in_b), custom_call_target="tpu_custom_call" | custom-call | tf_op jit(solution)/shard_map/store/pallas_call | solution.py:245

commit v5 on v4

--- a/solution.py
+++ b/solution.py
@@ -1,4 +1,3 @@
-import functools
 import random
 
 import jax
@@ -17,11 +16,44 @@
     return pltpu.with_memory_space_constraint(array, pltpu.HBM)
 
 
+def in_vmem(array):
+    return pltpu.with_memory_space_constraint(array, pltpu.VMEM)
+
+
 def far_first():
     offsets = [(dx, dy, dz) for dx in range(CHIPS) for dy in range(CHIPS) for dz in range(CHIPS)][1:]
     random.Random(1).shuffle(offsets)
     offsets.sort(key=lambda o: -sum(min(d, CHIPS - d) for d in o))
     return offsets
+
+
+def block(ref, side, k=None):
+    def column(c):
+        part = ref[side, :, c] if k is None else ref[side, :, c, k]
+        return part.reshape(128, 128)
+
+    return [jnp.concatenate([column(2 * j), column(2 * j + 1)], axis=1) for j in range(4)]
+
+
+def labels(mine, theirs):
+    return jnp.where(mine == theirs, 1.0, -1.0).astype(jnp.float32)
+
+
+def slope(mine, theirs, label, sharpness, shift):
+    score = jnp.zeros((128, 128), jnp.float32)
+    for p, q in zip(mine, theirs):
+        score += lax.dot_general(p, q, (((1,), (1,)), ((), ())), preferred_element_type=jnp.float32)
+    logit = sharpness * score + shift
+    return (-sharpness * label * jax.nn.sigmoid(-label * logit)).astype(jnp.bfloat16)
+
+
+def far_product(mine, theirs, label, sharpness, shift):
+    g = jnp.concatenate(
+        [slope(mine, t, label[k], sharpness, shift) for k, t in enumerate(theirs)], axis=1
+    )
+    for j in range(4):
+        slab = jnp.concatenate([t[j] for t in theirs], axis=0)
+        yield pl.ds(j * 256, 256), jnp.dot(g, slab, preferred_element_type=jnp.float32)
 
 
 def kernel(
@@ -34,13 +66,14 @@
     offset_ref,
     grad_a_ref,
     grad_b_ref,
+    own,
+    far,
+    label_ref,
     raw,
     ids,
     opponent_ref,
-    own,
     mid,
     out,
-    far,
     load_sem,
     send_sem,
     recv_sem,
@@ -117,20 +150,6 @@
     sharpness = sharpness_ref[0]
     shift = offset_ref[0]
 
-    def block(ref, side, k=None):
-        def column(c):
-            part = ref[side, :, c] if k is None else ref[side, :, c, k]
-            return part.reshape(128, 128)
-        return [jnp.concatenate([column(2 * j), column(2 * j + 1)], axis=1) for j in range(4)]
-
-    def slope(mine, theirs, my_ids, their_ids):
-        score = jnp.zeros((128, 128), jnp.float32)
-        for p, q in zip(mine, theirs):
-            score += lax.dot_general(p, q, (((1,), (1,)), ((), ())), preferred_element_type=jnp.float32)
-        label = jnp.where(my_ids == their_ids, 1.0, -1.0).astype(jnp.float32)
-        logit = sharpness * score + shift
-        return (-sharpness * label * jax.nn.sigmoid(-label * logit)).astype(jnp.bfloat16)
-
     for load in loads[2:]:
         load.wait()
     grads = (grad_a_ref, grad_b_ref)
@@ -140,9 +159,17 @@
         my_ids.append(jnp.transpose(jnp.broadcast_to(line, (128, 128))))
     for side in range(2):
         theirs = block(own, 1 - side)
-        g = slope(block(own, side), theirs, my_ids[side], ids[1 - side, pl.ds(me, 1), :])
+        label = labels(my_ids[side], ids[1 - side, pl.ds(me, 1), :])
+        g = slope(block(own, side), theirs, label, sharpness, shift)
         for j in range(4):
             grads[side][:, j * 256 : (j + 1) * 256] = jnp.dot(g, theirs[j], preferred_element_type=jnp.float32)
+
+    far_label = [
+        [labels(my_ids[side], ids[1 - side, pl.ds(opponent_ref[k, me], 1), :]) for k in range(rounds)]
+        for side in range(2)
+    ]
+    for k in range(rounds):
+        label_ref[k] = far_label[0][k]
 
     pltpu.make_async_copy(mid, mid, recv_sem.at[0]).wait()
 
@@ -164,21 +191,11 @@
     fetch(me)
     pltpu.make_async_copy(out.at[me], far.at[my_tile], recv_sem.at[1 + core]).start()
 
-    for side in (1, 0):
-        arrived = far.at[1 - side]
-        pltpu.make_async_copy(arrived, arrived, recv_sem.at[2 - side]).wait()
-        mine = block(own, side)
-        theirs = [block(far, 1 - side, k) for k in range(rounds)]
-        g = jnp.concatenate(
-            [
-                slope(mine, theirs[k], my_ids[side], ids[1 - side, pl.ds(opponent_ref[k, me], 1), :])
-                for k in range(rounds)
-            ],
-            axis=1,
-        )
-        for j in range(4):
-            slab = jnp.concatenate([theirs[k][j] for k in range(rounds)], axis=0)
-            grads[side][:, j * 256 : (j + 1) * 256] += jnp.dot(g, slab, preferred_element_type=jnp.float32)
+    pltpu.make_async_copy(far.at[0], far.at[0], recv_sem.at[1]).wait()
+    theirs = [block(far, 0, k) for k in range(rounds)]
+    for columns, product in far_product(block(own, 1), theirs, far_label[1], sharpness, shift):
+        grad_b_ref[:, columns] += product
+    pltpu.make_async_copy(far.at[1], far.at[1], recv_sem.at[2]).wait()
 
     spread_out = mid.at[pl.ds(0, len(spread))]
     pltpu.make_async_copy(spread_out, spread_out, send_sem.at[0]).wait()
@@ -186,13 +203,18 @@
     pltpu.make_async_copy(sent, sent, send_sem.at[1]).wait()
 
 
-def store(in_a, in_b, out_a, out_b, sem):
-    copies = [
-        pltpu.make_async_copy(src, dst, sem.at[side])
-        for side, (src, dst) in enumerate(((in_a, out_a), (in_b, out_b)))
-    ]
-    for copy in copies:
-        copy.start()
+def finish(sharpness_ref, offset_ref, part_a, grad_b, own, far, label_ref, out_a, out_b, total, sem):
+    copies = [pltpu.make_async_copy(grad_b, out_b, sem.at[4])]
+    copies[0].start()
+    rounds = label_ref.shape[0]
+    theirs = [block(far, 1, k) for k in range(rounds)]
+    label = [label_ref[k] for k in range(rounds)]
+    for j, (columns, product) in enumerate(
+        far_product(block(own, 0), theirs, label, sharpness_ref[0], offset_ref[0])
+    ):
+        total[:, columns] = part_a[:, columns] + product
+        copies.append(pltpu.make_async_copy(total.at[:, columns], out_a.at[:, columns], sem.at[j]))
+        copies[-1].start()
     for copy in copies:
         copy.wait()
 
@@ -212,19 +234,23 @@
     vmem = pl.BlockSpec(memory_space=pltpu.VMEM)
     smem = pl.BlockSpec(memory_space=pltpu.SMEM)
     grad = jax.ShapeDtypeStruct((rows, width), jnp.float32)
-    grads = pl.pallas_call(
+    parts = pl.pallas_call(
         kernel,
-        out_shape=(grad, grad),
+        out_shape=(
+            grad,
+            grad,
+            jax.ShapeDtypeStruct((2, 8, 8) + TILE, jnp.bfloat16),
+            jax.ShapeDtypeStruct((2, 8, 8, rounds) + TILE, jnp.bfloat16),
+            jax.ShapeDtypeStruct((rounds, rows, rows), jnp.float32),
+        ),
         in_specs=[hbm, hbm, hbm, hbm, hbm, smem, smem],
-        out_specs=(vmem, vmem),
+        out_specs=(vmem,) * 5,
         scratch_shapes=[
             pltpu.VMEM((2, rows, width), jnp.float32),
             pltpu.VMEM((2, blocks, rows), jnp.int32),
             pltpu.SMEM((rounds, blocks), jnp.int32),
-            pltpu.VMEM((2, 8, 8) + TILE, jnp.bfloat16),
             pltpu.VMEM((blocks,) + TILE, jnp.bfloat16),
             pltpu.VMEM((blocks, rounds) + TILE, jnp.bfloat16),
-            pltpu.VMEM((2, 8, 8, rounds) + TILE, jnp.bfloat16),
             pltpu.SemaphoreType.DMA((5,)),
             pltpu.SemaphoreType.DMA((2,)),
             pltpu.SemaphoreType.DMA((3,)),
@@ -243,13 +269,14 @@
         score_offset,
     )
     return pl.pallas_call(
-        store,
+        finish,
         out_shape=(grad, grad),
-        in_specs=[vmem, vmem],
+        in_specs=[smem, smem] + [vmem] * 5,
         out_specs=(hbm, hbm),
-        scratch_shapes=[pltpu.SemaphoreType.DMA((2,))],
-        name="store",
-    )(*[pltpu.with_memory_space_constraint(g, pltpu.VMEM) for g in grads])
+        scratch_shapes=[pltpu.VMEM((rows, width), jnp.float32), pltpu.SemaphoreType.DMA((5,))],
+        compiler_params=pltpu.CompilerParams(vmem_limit_bytes=16 * 1024 * 1024),
+        name="finish",
+    )(sharpness_array, score_offset, *[in_vmem(p) for p in parts])
 
 
 def solution(mesh):

time: 41 us -> 40.7 us (level)
  no operation moved by 1% of the time
where the time goes in v5:
time: 40.7 us; the launch traced here: 40.5 us
  Pallas kernels  38.6 us (95%)
  between operations  1.93 us (5%)
    pallas_call x1, Pallas kernels, shards(): pl.pallas_call(kernel, out_shape=(grad, grad, jax.ShapeDtypeStruct((2, 8,...  37.2 us
    pallas_call x1, Pallas kernels, shards(): pl.pallas_call(finish, out_shape=(grad, grad), in_specs=[smem, smem] + [v...  1.45 us

profile of v5, /device:TPU:0, one launch (start us, length us, event | category | flops | bytes accessed | tf_op | source)
XLA Modules:
  0.0 40.5 jit_solution(427557808334537913)
XLA Ops:
  1.9 37.2 %spread_deliver.1 = (f32[128,1024]{1,0:T(8,128)S(1)}, f32[128,1024]{1,0:T(8,128)S(1)}, bf16[2,8,8,16,128]{4,3,2,1,0:T(8,128)(2,1)S(1)}, bf16[2,8,8,3,16,128]{5,4,3,2,1,0:T(8,128)(2,1)S(1)}, f32[3,128,128]{2,1,0:T(8,128)S(1)}) custom-call(f32[128,1024]{1,0:T(8,128)} %a_ref.1, f32[128,1024]{1,0:T(8,128)} %b_ref.1, s32[128,128]{1,0:T(8,128)} %bitcast.2, ...), custom_call_target="tpu_custom_call" | custom-call | tf_op jit(solution)/shard_map/spread_deliver/pallas_call | solution.py:237
  39.1 1.4 %finish.1 = (f32[128,1024]{1,0:T(8,128)}, f32[128,1024]{1,0:T(8,128)}) custom-call(f32[1]{0:T(128)S(6)} %copy.9.sharpness_ref, f32[1]{0:T(128)S(6)} %copy.10.offset_ref, f32[128,1024]{1,0:T(8,128)S(1)} %get-tuple-element.7.part_a, f32[128,1024]{1,0:T(8,128)S(1)} %get-tuple-element.8.grad_b, bf16[2,8,8,16,128]{4,3,2,1,0:T(8,128)(2,1)S(1)} %get-tuple-element.9.own, ...), custom_call_target="tpu_custom_call" | custom-call | tf_op jit(solution)/shard_map/finish/pallas_call | solution.py:271

commit v6 on v5

--- a/solution.py
+++ b/solution.py
@@ -22,7 +22,7 @@
 
 def far_first():
     offsets = [(dx, dy, dz) for dx in range(CHIPS) for dy in range(CHIPS) for dz in range(CHIPS)][1:]
-    random.Random(1).shuffle(offsets)
+    random.Random(4).shuffle(offsets)
     offsets.sort(key=lambda o: -sum(min(d, CHIPS - d) for d in o))
     return offsets
 

time: 40.7 us -> 40.5 us (level)
  no operation moved by 1% of the time
where the time goes in v6:
time: 40.5 us; the launch traced here: 40.3 us
  Pallas kernels  38.4 us (95%)
  between operations  1.93 us (5%)
    pallas_call x1, Pallas kernels, shards(): pl.pallas_call(kernel, out_shape=(grad, grad, jax.ShapeDtypeStruct((2, 8,...  36.9 us
    pallas_call x1, Pallas kernels, shards(): pl.pallas_call(finish, out_shape=(grad, grad), in_specs=[smem, smem] + [v...  1.45 us

profile of v6, /device:TPU:0, one launch (start us, length us, event | category | flops | bytes accessed | tf_op | source)
XLA Modules:
  0.0 40.3 jit_solution(16436595193807979030)
XLA Ops:
  1.9 36.9 %spread_deliver.1 = (f32[128,1024]{1,0:T(8,128)S(1)}, f32[128,1024]{1,0:T(8,128)S(1)}, bf16[2,8,8,16,128]{4,3,2,1,0:T(8,128)(2,1)S(1)}, bf16[2,8,8,3,16,128]{5,4,3,2,1,0:T(8,128)(2,1)S(1)}, f32[3,128,128]{2,1,0:T(8,128)S(1)}) custom-call(f32[128,1024]{1,0:T(8,128)} %a_ref.1, f32[128,1024]{1,0:T(8,128)} %b_ref.1, s32[128,128]{1,0:T(8,128)} %bitcast.2, ...), custom_call_target="tpu_custom_call" | custom-call | tf_op jit(solution)/shard_map/spread_deliver/pallas_call | solution.py:237
  38.9 1.5 %finish.1 = (f32[128,1024]{1,0:T(8,128)}, f32[128,1024]{1,0:T(8,128)}) custom-call(f32[1]{0:T(128)S(6)} %copy.9.sharpness_ref, f32[1]{0:T(128)S(6)} %copy.10.offset_ref, f32[128,1024]{1,0:T(8,128)S(1)} %get-tuple-element.7.part_a, f32[128,1024]{1,0:T(8,128)S(1)} %get-tuple-element.8.grad_b, bf16[2,8,8,16,128]{4,3,2,1,0:T(8,128)(2,1)S(1)} %get-tuple-element.9.own, ...), custom_call_target="tpu_custom_call" | custom-call | tf_op jit(solution)/shard_map/finish/pallas_call | solution.py:271

commit v7 on v6

--- a/solution.py
+++ b/solution.py
@@ -119,7 +119,7 @@
     chips = far_first()
     here, beside = (0, 0, 0, core), (0, 0, 0, 1 - core)
     spread = [beside] + [o + (c,) for c in range(2) for o in chips]
-    deliver = [o + (c,) for c in (1, 0) for o in chips] + [beside]
+    deliver = [o + (c,) for _, c, o in sorted([(i + 36 * (c != 1), c, o) for i, o in enumerate(chips) for c in range(2)])] + [beside]
     barrier = pltpu.get_barrier_semaphore()
     for o in [o + (c,) for o in chips for c in range(2)] + [beside]:
         pl.semaphore_signal(barrier, inc=1, device_id=device(o), device_id_type=LOGICAL)
@@ -157,20 +157,6 @@
     for side in range(2):
         line = ids[side, pl.ds(me, 1), :]
         my_ids.append(jnp.transpose(jnp.broadcast_to(line, (128, 128))))
-    for side in range(2):
-        theirs = block(own, 1 - side)
-        label = labels(my_ids[side], ids[1 - side, pl.ds(me, 1), :])
-        g = slope(block(own, side), theirs, label, sharpness, shift)
-        for j in range(4):
-            grads[side][:, j * 256 : (j + 1) * 256] = jnp.dot(g, theirs[j], preferred_element_type=jnp.float32)
-
-    far_label = [
-        [labels(my_ids[side], ids[1 - side, pl.ds(opponent_ref[k, me], 1), :]) for k in range(rounds)]
-        for side in range(2)
-    ]
-    for k in range(rounds):
-        label_ref[k] = far_label[0][k]
-
     pltpu.make_async_copy(mid, mid, recv_sem.at[0]).wait()
 
     def fetch(there):
@@ -190,6 +176,22 @@
         ).start()
     fetch(me)
     pltpu.make_async_copy(out.at[me], far.at[my_tile], recv_sem.at[1 + core]).start()
+
+    far_label = [
+        [labels(my_ids[side], ids[1 - side, pl.ds(opponent_ref[k, me], 1), :]) for k in range(rounds)]
+        for side in range(2)
+    ]
+    for k in range(rounds):
+        label_ref[k] = far_label[0][k]
+
+
+    for side in range(2):
+        theirs = block(own, 1 - side)
+        label = labels(my_ids[side], ids[1 - side, pl.ds(me, 1), :])
+        g = slope(block(own, side), theirs, label, sharpness, shift)
+        for j in range(4):
+            grads[side][:, j * 256 : (j + 1) * 256] = jnp.dot(g, theirs[j], preferred_element_type=jnp.float32)
+
 
     pltpu.make_async_copy(far.at[0], far.at[0], recv_sem.at[1]).wait()
     theirs = [block(far, 0, k) for k in range(rounds)]

time: 40.5 us -> 40.5 us (level)
  no operation moved by 1% of the time
where the time goes in v7:
time: 40.5 us; the launch traced here: 40.3 us
  Pallas kernels  38.4 us (95%)
  between operations  1.93 us (5%)
    pallas_call x1, Pallas kernels, shards(): pl.pallas_call(kernel, out_shape=(grad, grad, jax.ShapeDtypeStruct((2, 8,...  36.9 us
    pallas_call x1, Pallas kernels, shards(): pl.pallas_call(finish, out_shape=(grad, grad), in_specs=[smem, smem] + [v...  1.45 us

profile of v7, /device:TPU:0, one launch (start us, length us, event | category | flops | bytes accessed | tf_op | source)
XLA Modules:
  0.0 40.3 jit_solution(235032385162195858)
XLA Ops:
  1.9 36.9 %spread_deliver.1 = (f32[128,1024]{1,0:T(8,128)S(1)}, f32[128,1024]{1,0:T(8,128)S(1)}, bf16[2,8,8,16,128]{4,3,2,1,0:T(8,128)(2,1)S(1)}, bf16[2,8,8,3,16,128]{5,4,3,2,1,0:T(8,128)(2,1)S(1)}, f32[3,128,128]{2,1,0:T(8,128)S(1)}) custom-call(f32[128,1024]{1,0:T(8,128)} %a_ref.1, f32[128,1024]{1,0:T(8,128)} %b_ref.1, s32[128,128]{1,0:T(8,128)} %bitcast.2, ...), custom_call_target="tpu_custom_call" | custom-call | tf_op jit(solution)/shard_map/spread_deliver/pallas_call | solution.py:239
  38.9 1.5 %finish.1 = (f32[128,1024]{1,0:T(8,128)}, f32[128,1024]{1,0:T(8,128)}) custom-call(f32[1]{0:T(128)S(6)} %copy.9.sharpness_ref, f32[1]{0:T(128)S(6)} %copy.10.offset_ref, f32[128,1024]{1,0:T(8,128)S(1)} %get-tuple-element.7.part_a, f32[128,1024]{1,0:T(8,128)S(1)} %get-tuple-element.8.grad_b, bf16[2,8,8,16,128]{4,3,2,1,0:T(8,128)(2,1)S(1)} %get-tuple-element.9.own, ...), custom_call_target="tpu_custom_call" | custom-call | tf_op jit(solution)/shard_map/finish/pallas_call | solution.py:273

commit v8 on v6

--- a/solution.py
+++ b/solution.py
@@ -77,6 +77,7 @@
     load_sem,
     send_sem,
     recv_sem,
+    entered,
 ):
     rounds = opponent_ref.shape[0]
     loads = [
@@ -118,10 +119,12 @@
 
     chips = far_first()
     here, beside = (0, 0, 0, core), (0, 0, 0, 1 - core)
-    spread = [beside] + [o + (c,) for c in range(2) for o in chips]
+    spread = [[o + (c,) for o in chips] for c in range(2)]
+    spread[1].append(beside)
     deliver = [o + (c,) for c in (1, 0) for o in chips] + [beside]
     barrier = pltpu.get_barrier_semaphore()
-    for o in [o + (c,) for o in chips for c in range(2)] + [beside]:
+    greeted = [o + (core,) for o in chips] + [beside]
+    for o in greeted:
         pl.semaphore_signal(barrier, inc=1, device_id=device(o), device_id_type=LOGICAL)
 
     for side in range(2):
@@ -133,17 +136,22 @@
             for c in range(8):
                 own[side, g, c] = value[:, c * 128 : (c + 1) * 128]
 
-    pl.semaphore_wait(barrier, len(deliver))
-
-    for o in spread:
-        pltpu.make_async_remote_copy(
-            src_ref=own.at[tile_of(o)],
-            dst_ref=mid.at[me],
-            send_sem=send_sem.at[0],
-            recv_sem=recv_sem.at[0],
-            device_id=device(o),
-            device_id_type=LOGICAL,
-        ).start()
+    pl.semaphore_wait(barrier, len(greeted))
+    pl.semaphore_signal(entered, inc=1, device_id=device(beside), device_id_type=LOGICAL)
+
+    for c in range(2):
+        @pl.when(core != c)
+        def _():
+            pl.semaphore_wait(entered, 1)
+        for o in spread[c]:
+            pltpu.make_async_remote_copy(
+                src_ref=own.at[tile_of(o)],
+                dst_ref=mid.at[me],
+                send_sem=send_sem.at[0],
+                recv_sem=recv_sem.at[0],
+                device_id=device(o),
+                device_id_type=LOGICAL,
+            ).start()
     my_tile = tile_of(here)
     pltpu.make_async_copy(own.at[my_tile], mid.at[me], recv_sem.at[0]).start()
 
@@ -197,7 +205,7 @@
         grad_b_ref[:, columns] += product
     pltpu.make_async_copy(far.at[1], far.at[1], recv_sem.at[2]).wait()
 
-    spread_out = mid.at[pl.ds(0, len(spread))]
+    spread_out = mid.at[pl.ds(0, len(deliver))]
     pltpu.make_async_copy(spread_out, spread_out, send_sem.at[0]).wait()
     sent = out.at[pl.ds(0, len(deliver))]
     pltpu.make_async_copy(sent, sent, send_sem.at[1]).wait()
@@ -254,6 +262,7 @@
             pltpu.SemaphoreType.DMA((5,)),
             pltpu.SemaphoreType.DMA((2,)),
             pltpu.SemaphoreType.DMA((3,)),
+            pltpu.SemaphoreType.REGULAR,
         ],
         compiler_params=pltpu.CompilerParams(
             collective_id=0, has_side_effects=True, vmem_limit_bytes=32 * 1024 * 1024

time: 40.5 us -> 40.5 us (level)
  no operation moved by 1% of the time
where the time goes in v8:
time: 40.5 us; the launch traced here: 40.3 us
  Pallas kernels  38.4 us (95%)
  between operations  1.93 us (5%)
    pallas_call x1, Pallas kernels, shards(): pl.pallas_call(kernel, out_shape=(grad, grad, jax.ShapeDtypeStruct((2, 8,...  36.9 us
    pallas_call x1, Pallas kernels, shards(): pl.pallas_call(finish, out_shape=(grad, grad), in_specs=[smem, smem] + [v...  1.44 us

profile of v8, /device:TPU:0, one launch (start us, length us, event | category | flops | bytes accessed | tf_op | source)
XLA Modules:
  0.0 40.3 jit_solution(545515458966211515)
XLA Ops:
  1.9 36.9 %spread_deliver.1 = (f32[128,1024]{1,0:T(8,128)S(1)}, f32[128,1024]{1,0:T(8,128)S(1)}, bf16[2,8,8,16,128]{4,3,2,1,0:T(8,128)(2,1)S(1)}, bf16[2,8,8,3,16,128]{5,4,3,2,1,0:T(8,128)(2,1)S(1)}, f32[3,128,128]{2,1,0:T(8,128)S(1)}) custom-call(f32[128,1024]{1,0:T(8,128)} %a_ref.1, f32[128,1024]{1,0:T(8,128)} %b_ref.1, s32[128,128]{1,0:T(8,128)} %bitcast.2, ...), custom_call_target="tpu_custom_call" | custom-call | tf_op jit(solution)/shard_map/spread_deliver/pallas_call | solution.py:245
  38.9 1.4 %finish.1 = (f32[128,1024]{1,0:T(8,128)}, f32[128,1024]{1,0:T(8,128)}) custom-call(f32[1]{0:T(128)S(6)} %copy.9.sharpness_ref, f32[1]{0:T(128)S(6)} %copy.10.offset_ref, f32[128,1024]{1,0:T(8,128)S(1)} %get-tuple-element.7.part_a, f32[128,1024]{1,0:T(8,128)S(1)} %get-tuple-element.8.grad_b, bf16[2,8,8,16,128]{4,3,2,1,0:T(8,128)(2,1)S(1)} %get-tuple-element.9.own, ...), custom_call_target="tpu_custom_call" | custom-call | tf_op jit(solution)/shard_map/finish/pallas_call | solution.py:280

commit v9 on v6

--- a/solution.py
+++ b/solution.py
@@ -119,7 +119,7 @@
     chips = far_first()
     here, beside = (0, 0, 0, core), (0, 0, 0, 1 - core)
     spread = [beside] + [o + (c,) for c in range(2) for o in chips]
-    deliver = [o + (c,) for c in (1, 0) for o in chips] + [beside]
+    deliver = [o + (c,) for _, c, o in sorted([(i + 36 * (c != 1), c, o) for i, o in enumerate(chips) for c in range(2)])] + [beside]
     barrier = pltpu.get_barrier_semaphore()
     for o in [o + (c,) for o in chips for c in range(2)] + [beside]:
         pl.semaphore_signal(barrier, inc=1, device_id=device(o), device_id_type=LOGICAL)

time: 40.5 us -> 40.5 us (level)
  no operation moved by 1% of the time
where the time goes in v9:
time: 40.5 us; the launch traced here: 40.3 us
  Pallas kernels  38.4 us (95%)
  between operations  1.93 us (5%)
    pallas_call x1, Pallas kernels, shards(): pl.pallas_call(kernel, out_shape=(grad, grad, jax.ShapeDtypeStruct((2, 8,...  36.9 us
    pallas_call x1, Pallas kernels, shards(): pl.pallas_call(finish, out_shape=(grad, grad), in_specs=[smem, smem] + [v...  1.45 us

profile of v9, /device:TPU:0, one launch (start us, length us, event | category | flops | bytes accessed | tf_op | source)
XLA Modules:
  0.0 40.3 jit_solution(10195486316552208483)
XLA Ops:
  1.9 36.9 %spread_deliver.1 = (f32[128,1024]{1,0:T(8,128)S(1)}, f32[128,1024]{1,0:T(8,128)S(1)}, bf16[2,8,8,16,128]{4,3,2,1,0:T(8,128)(2,1)S(1)}, bf16[2,8,8,3,16,128]{5,4,3,2,1,0:T(8,128)(2,1)S(1)}, f32[3,128,128]{2,1,0:T(8,128)S(1)}) custom-call(f32[128,1024]{1,0:T(8,128)} %a_ref.1, f32[128,1024]{1,0:T(8,128)} %b_ref.1, s32[128,128]{1,0:T(8,128)} %bitcast.2, ...), custom_call_target="tpu_custom_call" | custom-call | tf_op jit(solution)/shard_map/spread_deliver/pallas_call | solution.py:237
  38.9 1.5 %finish.1 = (f32[128,1024]{1,0:T(8,128)}, f32[128,1024]{1,0:T(8,128)}) custom-call(f32[1]{0:T(128)S(6)} %copy.9.sharpness_ref, f32[1]{0:T(128)S(6)} %copy.10.offset_ref, f32[128,1024]{1,0:T(8,128)S(1)} %get-tuple-element.7.part_a, f32[128,1024]{1,0:T(8,128)S(1)} %get-tuple-element.8.grad_b, bf16[2,8,8,16,128]{4,3,2,1,0:T(8,128)(2,1)S(1)} %get-tuple-element.9.own, ...), custom_call_target="tpu_custom_call" | custom-call | tf_op jit(solution)/shard_map/finish/pallas_call | solution.py:271
